TPU v7x, 128 devices: a whole 4x4x4 slice. The times are simulated.
128 devices in a mesh: occ: 8 (over y, core), vir: 16 (over z, x).
Axes of the slice: x: 4, y: 4, z: 4, core: 2. Of those that a mesh axis runs over, the one named last changes fastest.
Arguments:
- amplitude: bfloat16 [16, 640, 8, 640], P(None, 'vir'), may hold values from -6 to 6
- integral: bfloat16 [8, 640, 16, 640], P(None, 'vir', 'occ'), may hold values from -0.25 to 0.25
- occ_irrep: int32 [16], replicated, may hold values from 0 to 7
- kocc_irrep: int32 [8], replicated, may hold values from 0 to 7
- vir_irrep: int32 [640], replicated, may hold values from 0 to 7, as said below
Outputs:
- residual: bfloat16 [16, 640, 16, 640], P(None, 'vir', 'occ')
Inputs may be any that keep to these rules, and one draw needn't show every extreme that they name: `occ_irrep`: D2h irrep labels. `kocc_irrep`: D2h irrep labels. D2h irrep labels, ordered by irrep: vir_irrep never falls along the virtuals. The eight irreps hold, in an order that differs from draw to draw, 160, 120, three times 2 * 40 and three times 640 // 16 virtuals, so at most 160 virtuals share one irrep, and one irrep holds exactly that many.
All inputs are finite; a program needn't handle non-finite values.
Results may differ from a plain program's by a relative error of at most 0.0051.
Values may be sent and summed in bfloat16 or wider, within the bound.
A program may use at most 128 MiB of HBM per device.

v0:
```python
import functools
import jax
import jax.numpy as jnp
from jax import lax
from jax.experimental import pallas as pl
from jax.experimental.pallas import tpu as pltpu
from jax.sharding import PartitionSpec as P

WIN = 160
FEW = 6
MESH = pl.DeviceIdType.MESH
ORDER, PLACE, BEGIN, BLOCK, GROUP, MEMBER, MOST = 0, 16, 32, 40, 72, 88, 104


def table_kernel(groups, occ_ref, virs_ref, tab):
    batch = occ_ref.shape[0]
    la = virs_ref.shape[0] // 16
    occ = [occ_ref[i] for i in range(batch)]
    places = [jnp.int32(0)] * batch
    for i in range(batch):
        for o in range(i):
            before = (occ[o] <= occ[i]).astype(jnp.int32)
            places[i] = places[i] + before
            places[o] = places[o] + (1 - before)
    below = []
    for r in range(8):
        total = jnp.int32(0)
        for o in range(batch):
            total = total + (occ[o] < r).astype(jnp.int32)
        below.append(total)
    below.append(jnp.int32(batch))
    most = jnp.int32(0)
    for r in range(8):
        most = jnp.maximum(most, below[r + 1] - below[r])
        tab[BEGIN + r] = jnp.minimum(below[r], max(batch - 3 * groups, 0))
        for d in range(4):
            tab[BLOCK + 4 * r + d] = jnp.int32(0)
    for i in range(MOST, 128):
        tab[i] = most
    for v in range(16):
        tab[BLOCK + 4 * virs_ref[la * v] + v % 4] = jnp.int32(v)
    for i in range(batch):
        tab[PLACE + i] = places[i]
        tab[ORDER + places[i]] = jnp.int32(i)
        slot = places[i] - tab[BEGIN + occ[i]]
        group = jnp.int32(0)
        for q in range(1, groups):
            group = group + (slot >= 3 * q).astype(jnp.int32)
        tab[GROUP + i] = group
        tab[MEMBER + i] = slot - 3 * group


def make_table(groups, occ_irrep, vir_irrep):
    smem = pl.BlockSpec(memory_space=pltpu.SMEM)
    return pl.pallas_call(
        functools.partial(table_kernel, groups),
        out_shape=jax.ShapeDtypeStruct((128,), jnp.int32),
        in_specs=[smem, smem],
        out_specs=smem,
        name="make_table",
    )(occ_irrep, vir_irrep)


def cycle_kernel(groups, amp_ref, w_ref, occ_ref, kocc_ref, lab_ref, virs_ref, tab, out_ref,
                 amp, panels, tk, wk, acc, rowp, cw, comb, far, near, nearf, turned, pack_out, pack_in,
                 amp_sem, send_sem, recv_sem, far_send, far_recv, occ_send, occ_recv):
    me = lax.axis_index("vir")
    mine = lax.axis_index("occ")
    z, x = me // 4, lax.rem(me, 4)
    batch, la, nk, nv = amp.shape
    pairs = batch // 2
    here = [(x, z), (z, x)]

    amp_copies = [
        pltpu.make_async_copy(amp_ref.at[pl.ds(2 * i, 2)], amp.at[pl.ds(2 * i, 2)], amp_sem.at[i])
        for i in range(pairs)]
    for c in amp_copies:
        c.start()

    def at(h, p, q):
        p, q = lax.rem(p + 8, 4), lax.rem(q + 8, 4)
        return q * 4 + p if h == 0 else p * 4 + q

    def beside(off):
        return lax.rem(z + off // 4, 4) * 4 + lax.rem(x + lax.rem(off, 4), 4)

    def behind(off):
        return lax.rem(z + 4 - off // 4, 4) * 4 + lax.rem(x + 4 - lax.rem(off, 4), 4)

    barrier = pltpu.get_barrier_semaphore()

    @pl.loop(1, 16)
    def _(off):
        pl.semaphore_signal(barrier, inc=1, device_id={"vir": beside(off)}, device_id_type=MESH)

    @pl.loop(1, 8)
    def _(off):
        pl.semaphore_signal(barrier, inc=1, device_id={"occ": lax.rem(mine + off, 8)}, device_id_type=MESH)

    labs = lab_ref[...].reshape(1, nv)
    mylab = virs_ref[me * la]
    jocc = [occ_ref[2 * mine + j] for j in range(2)]

    quarter = lax.broadcasted_iota(jnp.int32, (la, nv), 1) // WIN

    def spread(part):
        part = part + pltpu.roll(part, 2 * WIN, 1)
        return part + pltpu.roll(part, WIN, 1)

    def pack(j):
        both = []
        for kp in range(2):
            total = None
            for kk in range(4):
                k = 4 * kp + kk
                want = kocc_ref[k] ^ jocc[j] ^ mylab
                part = spread(jnp.where(labs == want, w_ref[k, :, j, :].astype(jnp.float32), 0.0))
                total = part if total is None else jnp.where(quarter >= kk, part, total)
            both.append(total)
        panels[j, me] = jnp.concatenate(both, axis=0).astype(jnp.bfloat16)

    copies = []
    spans = [[(0, 48), (48, 80)], [(0, 32), (32, 80)]]

    def halves(j, h, turn):
        low, high = spans[j][h]
        middle = low + (32 if high - low == 48 and turn else 16)
        return (low, middle), (middle, high)

    def send(j, h, block, rows, step, slot):
        p, q = here[h]
        ref = panels.at[j, at(h, p + block[0], q + block[1]), pl.ds(rows[0], rows[1] - rows[0])]
        c = pltpu.make_async_remote_copy(
            src_ref=ref, dst_ref=ref, send_sem=send_sem.at[j, h, slot], recv_sem=recv_sem.at[j, h, slot],
            device_id={"vir": at(h, p + step[0], q + step[1])}, device_id_type=MESH)
        c.start()
        copies.append(c)

    def arrived(j, h, block, rows, slot):
        p, q = here[h]
        ref = panels.at[j, at(h, p + block[0], q + block[1]), pl.ds(rows[0], rows[1] - rows[0])]
        pltpu.make_async_remote_copy(
            src_ref=ref, dst_ref=ref, send_sem=send_sem.at[j, h, slot], recv_sem=recv_sem.at[j, h, slot],
            device_id={"vir": me}, device_id_type=MESH).wait_recv()

    def second(j, h, d):
        send(j, h, (d, 0), spans[j][h], (0, 1), 4 + 4 * d)
        send(j, h, (d, 0), spans[j][h], (0, -1), 5 + 4 * d)

    def start(j):
        for h in range(2):
            send(j, h, (0, 0), spans[j][h], (1, 0), 0)
            send(j, h, (0, 0), spans[j][h], (-1, 0), 1)
            second(j, h, 0)

    def first_axis(j):
        for h in range(2):
            low, high = halves(j, h, 0)
            arrived(j, h, (-1, 0), spans[j][h], 0)
            send(j, h, (-1, 0), low, (1, 0), 2)
            second(j, h, 3)
            arrived(j, h, (1, 0), spans[j][h], 1)
            send(j, h, (1, 0), high, (-1, 0), 3)
            second(j, h, 1)

    def opposite(j):
        for h in range(2):
            low, high = halves(j, h, 0)
            arrived(j, h, (-2, 0), low, 2)
            arrived(j, h, (-2, 0), high, 3)
            second(j, h, 2)

    def relay(j, d):
        b = d if d < 2 else d - 4
        for h in range(2):
            low, high = halves(j, h, d % 2)
            arrived(j, h, (b, -1), spans[j][h], 4 + 4 * d)
            send(j, h, (b, -1), low, (0, 1), 6 + 4 * d)
            arrived(j, h, (b, 1), spans[j][h], 5 + 4 * d)
            send(j, h, (b, 1), high, (0, -1), 7 + 4 * d)

    def complete(j):
        for h in range(2):
            for d in range(4):
                b = d if d < 2 else d - 4
                low, high = halves(j, h, d % 2)
                arrived(j, h, (b, 2), low, 6 + 4 * d)
                arrived(j, h, (b, 2), high, 7 + 4 * d)

    rows = la * nk

    def prepare(low, high):
        @pl.loop(low, high)
        def _(i):
            parts = []
            for s in range(2):
                orb = tab[ORDER + 2 * i + s]
                moved = jnp.dot(rowp[...], amp[orb].reshape(rows, nv), preferred_element_type=jnp.float32)
                left = occ_ref[orb] ^ mylab
                parts.append([
                    jnp.where(labs == (left ^ kocc_ref[k]), moved[k * la:(k + 1) * la], 0.0)
                    for k in range(nk)])
            for k in range(nk):
                tk[k, pl.ds(pl.multiple_of(2 * la * i, 16), 2 * la), :] = jnp.concatenate(
                    [parts[0][k], parts[1][k]], axis=0).astype(jnp.bfloat16)

    def order_rows(j):
        @pl.loop(0, 8)
        def _(v):
            one = panels[j, 2 * v].astype(jnp.float32)
            two = panels[j, 2 * v + 1].astype(jnp.float32)
            for kp in range(2):
                wk[j, kp, pl.ds(pl.multiple_of(2 * la * v, 16), 2 * la), :] = jnp.concatenate(
                    [one[kp * la:(kp + 1) * la], two[kp * la:(kp + 1) * la]], axis=0).astype(jnp.bfloat16)

    def multiply(j, low, high):
        @pl.loop(low, high)
        def _(kk):
            lanes = pl.ds(pl.multiple_of(128 * kk, 128), 256)
            t = jnp.concatenate([tk[kk], tk[4 + kk]], axis=1)
            w = jnp.concatenate([wk[j, 0, :, lanes], wk[j, 1, :, lanes]], axis=0)
            acc[kk] = jnp.dot(t, w, preferred_element_type=jnp.float32)

    def combine(j):
        whole = acc[0]
        for kk in range(1, 4):
            whole = whole + pltpu.roll(acc[kk], 256 - 32 * kk, 1)
        wide = lax.broadcasted_iota(jnp.int32, whole.shape, 1)
        whole = jnp.where(wide < WIN, whole, 0.0).astype(jnp.bfloat16).astype(jnp.float32)
        cw[j] = whole.reshape(batch, la, 256)
        spot = lax.broadcasted_iota(jnp.int32, (batch * la, 128), 1)
        for r in range(4):
            width = 128 if r < 3 else 256
            total = None
            for g in range(3):
                piece = whole[g * la:, :width]
                if g != r:
                    piece = pltpu.roll(piece, (la * (g - r)) % width, 1)
                piece = piece[:, :128]
                if g:
                    piece = jnp.concatenate([piece, jnp.zeros((g * la, 128), jnp.float32)], axis=0)
                total = piece if g == 0 else jnp.where(spot >= g * la, piece, total)
            comb[4 * j + r] = total.reshape(batch, la, 128)

    def message(j, v):
        base = tab[BEGIN + (jocc[j] ^ virs_ref[v * la] ^ mylab)]
        parts = [comb[4 * j + lax.rem(v, 4), base + 3 * q] for q in range(groups)]
        return jnp.concatenate(parts, axis=0).astype(jnp.bfloat16)

    def far_copy(j, off, v, source):
        return pltpu.make_async_remote_copy(
            src_ref=far.at[j, v], dst_ref=near.at[j, source], send_sem=far_send.at[j, off],
            recv_sem=far_recv.at[j, off], device_id={"vir": v}, device_id_type=MESH)

    def send_far(j):
        @pl.loop(1, 16)
        def _(off):
            v = beside(off)
            far[j, v] = message(j, v)
            far_copy(j, off, v, me).start()

    def take(j, source, value):
        nearf[source, groups * j:groups * (j + 1)] = value.astype(jnp.float32).reshape(groups, la, 128)

    def take_far(j):
        take(j, me, message(j, me))

        @pl.loop(1, 16)
        def _(off):
            source = behind(off)
            far_copy(j, off, source, source).wait_recv()
            take(j, source, near[j, source])

    def windows(j, o):
        wins = []
        for s in range(2):
            orb = 2 * o + s
            want = occ_ref[orb] ^ mylab ^ jocc[j]
            row = groups * j + tab[GROUP + orb]
            stack = [nearf[tab[BLOCK + 4 * want + d], row] for d in range(4)]
            stack = jnp.concatenate(stack + [jnp.zeros((96, 128), jnp.float32)], axis=0).T
            for m in range(3):
                turned[s, m] = stack[m * la:(m + 1) * la]
            wins.append(turned[s, tab[MEMBER + orb]])
        rest = wins[0][:, 128:] + pltpu.roll(wins[1][:, 128:], 32, 1)
        return jnp.concatenate(
            [wins[0][:, :128], wins[1][:, :128], rest, jnp.zeros((8, 128), jnp.float32)], axis=0).astype(jnp.bfloat16)

    def occ_copy(j, off, o, source):
        return pltpu.make_async_remote_copy(
            src_ref=pack_out.at[j, o], dst_ref=pack_in.at[j, source], send_sem=occ_send.at[j, off],
            recv_sem=occ_recv.at[j, off], device_id={"occ": o}, device_id_type=MESH)

    def send_occ(j):
        @pl.loop(1, 8)
        def _(off):
            o = lax.rem(mine + off, 8)
            pack_out[j, o] = windows(j, o)
            occ_copy(j, off, o, mine).start()

        pack_in[j, mine] = windows(j, mine)

    thin = lax.broadcasted_iota(jnp.int32, (la, 128), 1) < 32
    none = jnp.zeros((la, 128), jnp.float32)

    def finish(i2, o):
        orb = 2 * o + i2
        back = pack_in[i2, o].astype(jnp.float32)
        rest = back[2 * la:3 * la]
        for j in range(2):
            if j:
                rest = pltpu.roll(rest, 96, 1)
            own = cw[j, tab[PLACE + orb]]
            low = own[:, :128] + back[j * la:(j + 1) * la]
            high = own[:, 128:] + jnp.where(thin, rest, 0.0)
            row = spread(jnp.concatenate([low, high, none, none, none], axis=1))
            want = occ_ref[orb] ^ mylab ^ jocc[j]
            out_ref[orb, j] = jnp.where(labs == want, row, 0.0).astype(jnp.bfloat16)

    def finish_all(i2):
        finish(i2, mine)

        @pl.loop(1, 8)
        def _(off):
            source = lax.rem(mine + 8 - off, 8)
            occ_copy(i2, off, source, source).wait_recv()
            finish(i2, source)

    pack(0)
    pl.semaphore_wait(barrier, 22)
    start(0)
    pack(1)
    r = lax.broadcasted_iota(jnp.int32, (rows, rows), 0)
    c = lax.broadcasted_iota(jnp.int32, (rows, rows), 1)
    rowp[...] = (c == lax.rem(r, la) * nk + r // la).astype(jnp.float32).astype(jnp.bfloat16)
    for c in amp_copies:
        c.wait()
    first_axis(0)
    prepare(0, 2)
    relay(0, 0)
    opposite(0)
    prepare(2, 5)
    relay(0, 3)
    relay(0, 1)
    start(1)
    prepare(5, 8)
    relay(0, 2)
    first_axis(1)
    complete(0)
    order_rows(0)
    relay(1, 0)
    opposite(1)
    multiply(0, 0, 4)
    relay(1, 3)
    relay(1, 1)
    combine(0)
    send_far(0)
    relay(1, 2)
    complete(1)
    order_rows(1)
    multiply(1, 0, 4)
    combine(1)
    send_far(1)
    take_far(0)
    send_occ(0)
    take_far(1)
    send_occ(1)
    finish_all(0)
    finish_all(1)
    for c in copies:
        c.wait_send()
    for j in range(2):
        @pl.loop(1, 16)
        def _(off):
            far_copy(j, off, beside(off), me).wait_send()

        @pl.loop(1, 8)
        def _(off):
            occ_copy(j, off, lax.rem(mine + off, 8), mine).wait_send()


def residual_rows(groups, collective, amplitude, integral, occ_irrep, kocc_irrep, vir_irrep, table):
    batch, la, nk, nv = amplitude.shape
    rows = groups * la
    smem, vmem = pl.BlockSpec(memory_space=pltpu.SMEM), pl.BlockSpec(memory_space=pltpu.VMEM)
    return pl.pallas_call(
        functools.partial(cycle_kernel, groups),
        out_shape=jax.ShapeDtypeStruct((batch, 2, la, nv), jnp.bfloat16),
        in_specs=[pl.BlockSpec(memory_space=pl.ANY), vmem, smem, smem, vmem, smem, smem],
        out_specs=vmem,
        scratch_shapes=[
            pltpu.VMEM((batch, la, nk, nv), jnp.bfloat16),
            pltpu.VMEM((2, 16, 2 * la, 640), jnp.bfloat16),
            pltpu.VMEM((nk, batch * la, nv), jnp.bfloat16),
            pltpu.VMEM((2, 2, nv, 640), jnp.bfloat16),
            pltpu.VMEM((4, batch * la, 256), jnp.float32),
            pltpu.VMEM((la * nk, la * nk), jnp.bfloat16),
            pltpu.VMEM((2, batch, la, 256), jnp.float32),
            pltpu.VMEM((8, batch, la, 128), jnp.float32),
            pltpu.VMEM((2, 16, rows, 128), jnp.bfloat16),
            pltpu.VMEM((2, 16, rows, 128), jnp.bfloat16),
            pltpu.VMEM((16, 2 * groups, la, 128), jnp.float32),
            pltpu.VMEM((2, 3, la, 256), jnp.float32),
            pltpu.VMEM((2, 8, 128, 128), jnp.bfloat16),
            pltpu.VMEM((2, 8, 128, 128), jnp.bfloat16),
            pltpu.SemaphoreType.DMA((batch // 2,)),
            pltpu.SemaphoreType.DMA((2, 2, 20)),
            pltpu.SemaphoreType.DMA((2, 2, 20)),
            pltpu.SemaphoreType.DMA((2, 16)),
            pltpu.SemaphoreType.DMA((2, 16)),
            pltpu.SemaphoreType.DMA((2, 8)),
            pltpu.SemaphoreType.DMA((2, 8)),
        ],
        compiler_params=pltpu.CompilerParams(
            collective_id=collective, has_side_effects=True, vmem_limit_bytes=56 * 1024 * 1024),
        name="cycle_residual",
    )(amplitude, integral, occ_irrep, kocc_irrep, vir_irrep, vir_irrep, table)


def shards(amplitude, integral, occ_irrep, kocc_irrep, vir_irrep):
    table = make_table(2, occ_irrep, vir_irrep)
    args = (amplitude, integral, occ_irrep, kocc_irrep, vir_irrep)
    rows = lax.cond(
        table[MOST] <= FEW,
        lambda *a: residual_rows(2, 0, *a, table),
        lambda *a: residual_rows(6, 1, *a, make_table(6, occ_irrep, vir_irrep)),
        *args,
    )
    return jnp.transpose(rows, (0, 2, 1, 3))


def solution(mesh):
    in_specs = (P(None, "vir", None, None), P(None, "vir", "occ", None), P(), P(), P())
    out_specs = P(None, "vir", "occ", None)
    return jax.shard_map(shards, mesh=mesh, in_specs=in_specs, out_specs=out_specs, check_vma=False)
```

profile of v0, /device:TPU:1, one launch (start us, length us, event | category | flops | bytes accessed | tf_op | source)
XLA Modules:
  0.0 62.9 jit_solution(11224564947577257314)
XLA Ops:
  0.0 1.8 %make_table.3 = s32[128]{0:T(128)S(1)} custom-call(s32[16]{0:T(128)} %occ_ref.1, s32[640]{0:T(1024)} %virs_ref.1), custom_call_target="tpu_custom_call" | custom-call | tf_op jit(solution)/shard_map/make_table/pallas_call | solution.py:55
  1.8 0.6 slice.3
  3.1 57.4 %conditional.1 = (bf16[16,2,40,640]{3,2,1,0:T(8,128)(2,1)S(1)}) conditional(s32[]{:T(128)} %bitcast, (s32[16]{0:T(128)}, s32[640]{0:T(1024)}, bf16[16,40,8,640]{3,2,1,0:T(8,128)(2,1)}, bf16[8,40,2,640]{3,2,1,0:T(2,128)(2,1)}, s32[8]{0:T(128)}) %tuple.11, (bf16[16,40,8,640]{3,2,1,0:T(8,128)(2,1)}, bf16[8,40,2,640]{3,2,1,0:T(2,128)(2,1)}, s32[16]{0:T(128)}, ...), branch_computations={%region_0.0_spmd, %region_1.0_spmd} | conditional | bytes 8 | solution.py:423
  3.3 57.2 %cycle_residual.3 = bf16[16,2,40,640]{3,2,1,0:T(8,128)(2,1)S(1)} custom-call(bf16[16,40,8,640]{3,2,1,0:T(8,128)(2,1)} %get-tuple-element.35.amp_ref, bf16[8,40,2,640]{3,2,1,0:T(2,128)(2,1)} %get-tuple-element.36.w_ref, s32[16]{0:T(128)} %get-tuple-element.37.occ_ref, s32[8]{0:T(128)} %get-tuple-element.38.kocc_ref, s32[640]{0:T(1024)} %get-tuple-element.39.lab_ref.virs_ref, ...), custom_call_target="tpu_custom_call" | custom-call | tf_op jit(solution)/shard_map/cond/branch_1_fun/cycle_residual/pallas_call | solution.py:386
  60.5 2.4 %copy.8 = bf16[16,2,40,640]{3,1,2,0:T(2,128)(2,1)} copy(bf16[16,2,40,640]{3,2,1,0:T(8,128)(2,1)S(1)} %get-tuple-element.41) | data formatting | bytes 3276800 | tf_op jit(solution)/shard_map/cond | solution.py:423
where the time goes:
time: 63 us; the launch traced here: 62.9 us
  Pallas kernels  59 us (94%)
  local copies, waits for them, and re-layouts  3.01 us (5%)
  between operations  0.67 us (1%)
    pallas_call x1, Pallas kernels, residual_rows(): pl.pallas_call(functools.partial(cycle_kernel, groups), out_shape=jax.Sha...  57.2 us
    cond x1, local copies, waits for them, and re-layouts, shards(): lax.cond(table[MOST] <= FEW, lambda *a: residual_rows(2, 0, *a, table), l...  2.43 us
    pallas_call x1, Pallas kernels, make_table(): pl.pallas_call(functools.partial(table_kernel, groups), out_shape=jax.Sha...  1.82 us

commit v1 on v0

v1 whole, which is shorter than its diff:
```python
import functools
import jax
import jax.numpy as jnp
from jax import lax
from jax.experimental import pallas as pl
from jax.experimental.pallas import tpu as pltpu
from jax.sharding import PartitionSpec as P

WIN = 160
FEW, FEW_ODD = 6, 3
MESH = pl.DeviceIdType.MESH
ORDER, PLACE, BEGIN, BLOCK, GROUP, MEMBER, MOST = 0, 16, 32, 40, 72, 88, 104
ODD_ORDER, ODD_BEGIN, ODD_GROUP, ODD_MEMBER = 128, 136, 144, 152


def table_kernel(groups, occ_ref, virs_ref, tab):
    batch = occ_ref.shape[0]
    la = virs_ref.shape[0] // 16
    occ = [occ_ref[i] for i in range(batch)]
    places = [jnp.int32(0)] * batch
    for i in range(batch):
        for o in range(i):
            before = (occ[o] <= occ[i]).astype(jnp.int32)
            places[i] = places[i] + before
            places[o] = places[o] + (1 - before)
    below = []
    for r in range(8):
        total = jnp.int32(0)
        for o in range(batch):
            total = total + (occ[o] < r).astype(jnp.int32)
        below.append(total)
    below.append(jnp.int32(batch))
    odd_below = []
    for r in range(8):
        total = jnp.int32(0)
        for o in range(1, batch, 2):
            total = total + (occ[o] < r).astype(jnp.int32)
        odd_below.append(total)
    odd_below.append(jnp.int32(batch // 2))
    odd_groups = groups // 2
    excess = jnp.int32(0)
    for r in range(8):
        excess = jnp.maximum(excess, below[r + 1] - below[r] - FEW)
        excess = jnp.maximum(excess, odd_below[r + 1] - odd_below[r] - FEW_ODD)
        tab[BEGIN + r] = jnp.minimum(below[r], max(batch - 3 * groups, 0))
        tab[ODD_BEGIN + r] = jnp.minimum(odd_below[r], max(batch // 2 - 3 * odd_groups, 0))
        for d in range(4):
            tab[BLOCK + 4 * r + d] = jnp.int32(0)
    for i in range(MOST, 128):
        tab[i] = excess
    for v in range(16):
        tab[BLOCK + 4 * virs_ref[la * v] + v % 4] = jnp.int32(v)

    def enter(slot, count, group_at, member_at):
        group = jnp.int32(0)
        for q in range(1, count):
            group = group + (slot >= 3 * q).astype(jnp.int32)
        tab[group_at] = group
        tab[member_at] = slot - 3 * group

    for i in range(batch):
        tab[PLACE + i] = places[i]
        tab[ORDER + places[i]] = jnp.int32(i)
        enter(places[i] - tab[BEGIN + occ[i]], groups, GROUP + i, MEMBER + i)
    for t in range(batch // 2):
        place = jnp.int32(0)
        for o in range(batch // 2):
            if o != t:
                a, b = occ[2 * o + 1], occ[2 * t + 1]
                place = place + ((a <= b) if o < t else (a < b)).astype(jnp.int32)
        tab[ODD_ORDER + place] = jnp.int32(t)
        enter(place - tab[ODD_BEGIN + occ[2 * t + 1]], odd_groups, ODD_GROUP + t, ODD_MEMBER + t)
    for i in range(160, 256):
        tab[i] = jnp.int32(0)


def make_table(groups, occ_irrep, vir_irrep):
    smem = pl.BlockSpec(memory_space=pltpu.SMEM)
    return pl.pallas_call(
        functools.partial(table_kernel, groups),
        out_shape=jax.ShapeDtypeStruct((256,), jnp.int32),
        in_specs=[smem, smem],
        out_specs=smem,
        name="make_table",
    )(occ_irrep, vir_irrep)


def cycle_kernel(groups, amp_ref, w_ref, occ_ref, kocc_ref, lab_ref, virs_ref, tab, out_ref,
                 amp, panels, tk, wk, acc, rowp, cw, comb, far, near, nearf, turned, pack_out, pack_in, odd, odd_comb,
                 amp_sem, send_sem, recv_sem, far_send, far_recv, occ_send, occ_recv):
    me = lax.axis_index("vir")
    mine = lax.axis_index("occ")
    z, x = me // 4, lax.rem(me, 4)
    batch, la, nk, nv = amp.shape
    pairs = batch // 2
    here = [(x, z), (z, x)]

    amp_copies = [
        pltpu.make_async_copy(amp_ref.at[pl.ds(2 * i, 2)], amp.at[pl.ds(2 * i, 2)], amp_sem.at[i])
        for i in range(pairs)]
    for c in amp_copies:
        c.start()

    def at(h, p, q):
        p, q = lax.rem(p + 8, 4), lax.rem(q + 8, 4)
        return q * 4 + p if h == 0 else p * 4 + q

    def beside(off):
        return lax.rem(z + off // 4, 4) * 4 + lax.rem(x + lax.rem(off, 4), 4)

    def behind(off):
        return lax.rem(z + 4 - off // 4, 4) * 4 + lax.rem(x + 4 - lax.rem(off, 4), 4)

    barrier = pltpu.get_barrier_semaphore()

    @pl.loop(1, 16)
    def _(off):
        pl.semaphore_signal(barrier, inc=1, device_id={"vir": beside(off)}, device_id_type=MESH)

    @pl.loop(1, 8)
    def _(off):
        pl.semaphore_signal(barrier, inc=1, device_id={"occ": lax.rem(mine + off, 8)}, device_id_type=MESH)

    labs = lab_ref[...].reshape(1, nv)
    mylab = virs_ref[me * la]
    jocc = [occ_ref[2 * mine + j] for j in range(2)]

    quarter = lax.broadcasted_iota(jnp.int32, (la, nv), 1) // WIN

    def spread(part):
        part = part + pltpu.roll(part, 2 * WIN, 1)
        return part + pltpu.roll(part, WIN, 1)

    def pack(j):
        both = []
        for kp in range(2):
            total = None
            for kk in range(4):
                k = 4 * kp + kk
                want = kocc_ref[k] ^ jocc[j] ^ mylab
                part = spread(jnp.where(labs == want, w_ref[k, :, j, :].astype(jnp.float32), 0.0))
                total = part if total is None else jnp.where(quarter >= kk, part, total)
            both.append(total)
        panels[j, me] = jnp.concatenate(both, axis=0).astype(jnp.bfloat16)

    copies = []
    full = (0, 2 * la)

    def halves(h, turn):
        middle = 48 if (h + turn) % 2 else 32
        return (0, middle), (middle, 2 * la)

    def send(h, block, rows, step, slot):
        p, q = here[h]
        ref = panels.at[h, at(h, p + block[0], q + block[1]), pl.ds(rows[0], rows[1] - rows[0])]
        c = pltpu.make_async_remote_copy(
            src_ref=ref, dst_ref=ref, send_sem=send_sem.at[h, slot], recv_sem=recv_sem.at[h, slot],
            device_id={"vir": at(h, p + step[0], q + step[1])}, device_id_type=MESH)
        c.start()
        copies.append(c)

    def arrived(h, block, rows, slot):
        p, q = here[h]
        ref = panels.at[h, at(h, p + block[0], q + block[1]), pl.ds(rows[0], rows[1] - rows[0])]
        pltpu.make_async_remote_copy(
            src_ref=ref, dst_ref=ref, send_sem=send_sem.at[h, slot], recv_sem=recv_sem.at[h, slot],
            device_id={"vir": me}, device_id_type=MESH).wait_recv()

    def second(h, d):
        send(h, (d, 0), full, (0, 1), 4 + 4 * d)
        send(h, (d, 0), full, (0, -1), 5 + 4 * d)

    def start(h):
        send(h, (0, 0), full, (1, 0), 0)
        send(h, (0, 0), full, (-1, 0), 1)
        second(h, 0)

    def first_axis():
        for h in range(2):
            low, high = halves(h, 0)
            arrived(h, (-1, 0), full, 0)
            send(h, (-1, 0), low, (1, 0), 2)
            second(h, 3)
            arrived(h, (1, 0), full, 1)
            send(h, (1, 0), high, (-1, 0), 3)
            second(h, 1)

    def opposite():
        for h in range(2):
            low, high = halves(h, 0)
            arrived(h, (-2, 0), low, 2)
            arrived(h, (-2, 0), high, 3)
            second(h, 2)

    def relay(d):
        b = d if d < 2 else d - 4
        for h in range(2):
            low, high = halves(h, d % 2)
            arrived(h, (b, -1), full, 4 + 4 * d)
            send(h, (b, -1), low, (0, 1), 6 + 4 * d)
            arrived(h, (b, 1), full, 5 + 4 * d)
            send(h, (b, 1), high, (0, -1), 7 + 4 * d)

    def complete(h):
        for d in range(4):
            b = d if d < 2 else d - 4
            low, high = halves(h, d % 2)
            arrived(h, (b, 2), low, 6 + 4 * d)
            arrived(h, (b, 2), high, 7 + 4 * d)

    rows = la * nk

    def prepare(low, high):
        @pl.loop(low, high)
        def _(i):
            parts = []
            for s in range(2):
                orb = tab[ORDER + 2 * i + s]
                moved = jnp.dot(rowp[...], amp[orb].reshape(rows, nv), preferred_element_type=jnp.float32)
                left = occ_ref[orb] ^ mylab
                parts.append([
                    jnp.where(labs == (left ^ kocc_ref[k]), moved[k * la:(k + 1) * la], 0.0)
                    for k in range(nk)])
            for k in range(nk):
                tk[k, pl.ds(pl.multiple_of(2 * la * i, 16), 2 * la), :] = jnp.concatenate(
                    [parts[0][k], parts[1][k]], axis=0).astype(jnp.bfloat16)

    def order_rows(j):
        @pl.loop(0, 8)
        def _(v):
            one = panels[j, 2 * v].astype(jnp.float32)
            two = panels[j, 2 * v + 1].astype(jnp.float32)
            for kp in range(2):
                wk[j, kp, pl.ds(pl.multiple_of(2 * la * v, 16), 2 * la), :] = jnp.concatenate(
                    [one[kp * la:(kp + 1) * la], two[kp * la:(kp + 1) * la]], axis=0).astype(jnp.bfloat16)

    def multiply(j, low, high):
        @pl.loop(low, high)
        def _(kk):
            lanes = pl.ds(pl.multiple_of(128 * kk, 128), 256)
            t = jnp.concatenate([tk[kk], tk[4 + kk]], axis=1)
            w = jnp.concatenate([wk[j, 0, :, lanes], wk[j, 1, :, lanes]], axis=0)
            acc[kk] = jnp.dot(t, w, preferred_element_type=jnp.float32)

    def collect(j):
        whole = acc[0]
        for kk in range(1, 4):
            whole = whole + pltpu.roll(acc[kk], 256 - 32 * kk, 1)
        wide = lax.broadcasted_iota(jnp.int32, whole.shape, 1)
        whole = jnp.where(wide < WIN, whole, 0.0).astype(jnp.bfloat16).astype(jnp.float32)
        cw[j] = whole.reshape(batch, la, 256)
        return whole

    def mix(whole, r):
        spot = lax.broadcasted_iota(jnp.int32, (whole.shape[0], 128), 1)
        width = 128 if r < 3 else 256
        total = None
        for g in range(3):
            piece = whole[g * la:, :width]
            if g != r:
                piece = pltpu.roll(piece, (la * (g - r)) % width, 1)
            piece = piece[:, :128]
            if g:
                piece = jnp.concatenate([piece, jnp.zeros((g * la, 128), jnp.float32)], axis=0)
            total = piece if g == 0 else jnp.where(spot >= g * la, piece, total)
        return total.reshape(whole.shape[0] // la, la, 128)

    def even_message(v):
        base = tab[BEGIN + (jocc[0] ^ virs_ref[v * la] ^ mylab)]
        parts = [comb[lax.rem(v, 4), base + 3 * q] for q in range(groups)]
        return jnp.concatenate(parts, axis=0).astype(jnp.bfloat16)

    def odd_message(v):
        parts = []
        for s in range(2):
            base = tab[ODD_BEGIN + (jocc[s] ^ virs_ref[v * la] ^ mylab)]
            parts += [odd_comb[4 * s + lax.rem(v, 4), base + 3 * q] for q in range(groups // 2)]
        return jnp.concatenate(parts, axis=0).astype(jnp.bfloat16)

    messages = [even_message, odd_message]

    def far_copy(j, off, v, source):
        return pltpu.make_async_remote_copy(
            src_ref=far.at[j, v], dst_ref=near.at[j, source], send_sem=far_send.at[j, off],
            recv_sem=far_recv.at[j, off], device_id={"vir": v}, device_id_type=MESH)

    def send_far(j):
        @pl.loop(1, 16)
        def _(off):
            v = beside(off)
            far[j, v] = messages[j](v)
            far_copy(j, off, v, me).start()

    def take(j, source, value):
        nearf[j, source] = value.astype(jnp.float32).reshape(groups, la, 128)

    def take_far(j):
        take(j, me, messages[j](me))

        @pl.loop(1, 16)
        def _(off):
            source = behind(off)
            far_copy(j, off, source, source).wait_recv()
            take(j, source, near[j, source])

    def window(j, s, want, row, member):
        stack = [nearf[j, tab[BLOCK + 4 * want + d], row] for d in range(4)]
        stack = jnp.concatenate(stack + [jnp.zeros((96, 128), jnp.float32)], axis=0).T
        for m in range(3):
            turned[s, m] = stack[m * la:(m + 1) * la]
        return turned[s, member]

    def join(wins):
        rest = wins[0][:, 128:] + pltpu.roll(wins[1][:, 128:], 32, 1)
        return jnp.concatenate(
            [wins[0][:, :128], wins[1][:, :128], rest, jnp.zeros((8, 128), jnp.float32)], axis=0).astype(jnp.bfloat16)

    def even_windows(o):
        wins = []
        for s in range(2):
            orb = 2 * o + s
            wins.append(window(0, s, occ_ref[orb] ^ mylab ^ jocc[0], tab[GROUP + orb], tab[MEMBER + orb]))
        return join(wins)

    def odd_windows(o):
        return join([cw[1, tab[PLACE + 2 * o + s]] for s in range(2)])

    def occ_copy(j, off, o, source):
        return pltpu.make_async_remote_copy(
            src_ref=pack_out.at[j, o], dst_ref=pack_in.at[j, source], send_sem=occ_send.at[j, off],
            recv_sem=occ_recv.at[j, off], device_id={"occ": o}, device_id_type=MESH)

    def send_occ(j, make):
        @pl.loop(1, 8)
        def _(off):
            o = lax.rem(mine + off, 8)
            pack_out[j, o] = make(o)
            occ_copy(j, off, o, mine).start()

        pack_in[j, mine] = make(mine)

    thin = lax.broadcasted_iota(jnp.int32, (la, 128), 1) < 32
    none = jnp.zeros((la, 128), jnp.float32)

    def part_of(j, o):
        back = pack_in[j, o].astype(jnp.float32)
        rest = back[2 * la:3 * la]
        return [
            jnp.concatenate([back[:la], jnp.where(thin, rest, 0.0)], axis=1),
            jnp.concatenate([back[la:2 * la], jnp.where(thin, pltpu.roll(rest, 96, 1), 0.0)], axis=1)]

    def wait_occ(j, then):
        then(mine)

        @pl.loop(1, 8)
        def _(off):
            source = lax.rem(mine + 8 - off, 8)
            occ_copy(j, off, source, source).wait_recv()
            then(source)

    def finish(orb, mirrors):
        for j in range(2):
            row = cw[j, tab[PLACE + orb]] + mirrors[j]
            row = spread(jnp.concatenate([row, none, none, none], axis=1))
            want = occ_ref[orb] ^ mylab ^ jocc[j]
            out_ref[orb, j] = jnp.where(labs == want, row, 0.0).astype(jnp.bfloat16)

    def keep_odd(o):
        odd[0, o], odd[1, o] = part_of(1, o)

    def finish_odd():
        @pl.loop(0, 8)
        def _(o):
            orb = 2 * o + 1
            finish(orb, [
                window(1, s, occ_ref[orb] ^ mylab ^ jocc[s], groups // 2 * s + tab[ODD_GROUP + o], tab[ODD_MEMBER + o])
                for s in range(2)])

    pack(0)
    pl.semaphore_wait(barrier, 22)
    start(0)
    pack(1)
    start(1)
    r = lax.broadcasted_iota(jnp.int32, (rows, rows), 0)
    c = lax.broadcasted_iota(jnp.int32, (rows, rows), 1)
    rowp[...] = (c == lax.rem(r, la) * nk + r // la).astype(jnp.float32).astype(jnp.bfloat16)
    for c in amp_copies:
        c.wait()
    prepare(0, 1)
    first_axis()
    prepare(1, 2)
    relay(0)
    prepare(2, 3)
    opposite()
    prepare(3, 5)
    relay(3)
    prepare(5, 6)
    relay(1)
    prepare(6, 8)
    relay(2)
    complete(1)
    order_rows(1)
    multiply(1, 0, 4)
    collect(1)
    send_occ(1, odd_windows)
    complete(0)
    order_rows(0)
    multiply(0, 0, 4)
    whole = collect(0)
    for q in range(4):
        comb[q] = mix(whole, q)
    send_far(0)

    wait_occ(1, keep_odd)
    for s in range(2):
        sorted_odd = jnp.concatenate([odd[s, tab[ODD_ORDER + t]] for t in range(batch // 2)], axis=0)
        for q in range(4):
            odd_comb[4 * s + q] = mix(sorted_odd, q)
    send_far(1)
    take_far(0)
    send_occ(0, even_windows)
    take_far(1)
    finish_odd()
    wait_occ(0, lambda o: finish(2 * o, part_of(0, o)))
    for c in copies:
        c.wait_send()
    for j in range(2):
        @pl.loop(1, 16)
        def _(off):
            far_copy(j, off, beside(off), me).wait_send()

        @pl.loop(1, 8)
        def _(off):
            occ_copy(j, off, lax.rem(mine + off, 8), mine).wait_send()


def residual_rows(groups, collective, amplitude, integral, occ_irrep, kocc_irrep, vir_irrep, table):
    batch, la, nk, nv = amplitude.shape
    rows = groups * la
    smem, vmem = pl.BlockSpec(memory_space=pltpu.SMEM), pl.BlockSpec(memory_space=pltpu.VMEM)
    return pl.pallas_call(
        functools.partial(cycle_kernel, groups),
        out_shape=jax.ShapeDtypeStruct((batch, 2, la, nv), jnp.bfloat16),
        in_specs=[pl.BlockSpec(memory_space=pl.ANY), vmem, smem, smem, vmem, smem, smem],
        out_specs=vmem,
        scratch_shapes=[
            pltpu.VMEM((batch, la, nk, nv), jnp.bfloat16),
            pltpu.VMEM((2, 16, 2 * la, 640), jnp.bfloat16),
            pltpu.VMEM((nk, batch * la, nv), jnp.bfloat16),
            pltpu.VMEM((2, 2, nv, 640), jnp.bfloat16),
            pltpu.VMEM((4, batch * la, 256), jnp.float32),
            pltpu.VMEM((la * nk, la * nk), jnp.bfloat16),
            pltpu.VMEM((2, batch, la, 256), jnp.float32),
            pltpu.VMEM((4, batch, la, 128), jnp.float32),
            pltpu.VMEM((2, 16, rows, 128), jnp.bfloat16),
            pltpu.VMEM((2, 16, rows, 128), jnp.bfloat16),
            pltpu.VMEM((2, 16, groups, la, 128), jnp.float32),
            pltpu.VMEM((2, 3, la, 256), jnp.float32),
            pltpu.VMEM((2, 8, 128, 128), jnp.bfloat16),
            pltpu.VMEM((2, 8, 128, 128), jnp.bfloat16),
            pltpu.VMEM((2, 8, la, 256), jnp.float32),
            pltpu.VMEM((8, 8, la, 128), jnp.float32),
            pltpu.SemaphoreType.DMA((batch // 2,)),
            pltpu.SemaphoreType.DMA((2, 20)),
            pltpu.SemaphoreType.DMA((2, 20)),
            pltpu.SemaphoreType.DMA((2, 16)),
            pltpu.SemaphoreType.DMA((2, 16)),
            pltpu.SemaphoreType.DMA((2, 8)),
            pltpu.SemaphoreType.DMA((2, 8)),
        ],
        compiler_params=pltpu.CompilerParams(
            collective_id=collective, has_side_effects=True, vmem_limit_bytes=56 * 1024 * 1024),
        name="cycle_residual",
    )(amplitude, integral, occ_irrep, kocc_irrep, vir_irrep, vir_irrep, table)


def shards(amplitude, integral, occ_irrep, kocc_irrep, vir_irrep):
    table = make_table(2, occ_irrep, vir_irrep)
    args = (amplitude, integral, occ_irrep, kocc_irrep, vir_irrep)
    rows = lax.cond(
        table[MOST] <= 0,
        lambda *a: residual_rows(2, 0, *a, table),
        lambda *a: residual_rows(6, 1, *a, make_table(6, occ_irrep, vir_irrep)),
        *args,
    )
    return jnp.transpose(rows, (0, 2, 1, 3))


def solution(mesh):
    in_specs = (P(None, "vir", None, None), P(None, "vir", "occ", None), P(), P(), P())
    out_specs = P(None, "vir", "occ", None)
    return jax.shard_map(shards, mesh=mesh, in_specs=in_specs, out_specs=out_specs, check_vma=False)
```

time: 63 us -> 60.6 us (0.962)
  Pallas kernels: 59 us -> 56.6 us
    pallas_call x1, Pallas kernels: 57.2 us -> 54.6 us  [residual_rows(): pl.pallas_call(functools.partial(cycle_kernel, groups), out_shape=jax.Sha...]
where the time goes in v1:
time: 60.6 us; the launch traced here: 60.5 us
  Pallas kernels  56.6 us (93%)
  local copies, waits for them, and re-layouts  3.01 us (5%)
  between operations  0.67 us (1%)
    pallas_call x1, Pallas kernels, residual_rows(): pl.pallas_call(functools.partial(cycle_kernel, groups), out_shape=jax.Sha...  54.6 us
    cond x1, local copies, waits for them, and re-layouts, shards(): lax.cond(table[MOST] <= 0, lambda *a: residual_rows(2, 0, *a, table), lam...  2.43 us
    pallas_call x1, Pallas kernels, make_table(): pl.pallas_call(functools.partial(table_kernel, groups), out_shape=jax.Sha...  2.01 us

profile of v1, /device:TPU:1, one launch (start us, length us, event | category | flops | bytes accessed | tf_op | source)
XLA Modules:
  0.0 60.5 jit_solution(9835194094323609677)
XLA Ops:
  0.0 2.0 %make_table.3 = s32[256]{0:T(256)S(1)} custom-call(s32[16]{0:T(128)} %occ_ref.1, s32[640]{0:T(1024)} %virs_ref.1), custom_call_target="tpu_custom_call" | custom-call | tf_op jit(solution)/shard_map/make_table/pallas_call | solution.py:79
  2.0 0.6 slice.3
  3.2 54.8 %conditional.1 = (bf16[16,2,40,640]{3,2,1,0:T(8,128)(2,1)S(1)}) conditional(s32[]{:T(128)} %bitcast, (s32[16]{0:T(128)}, s32[640]{0:T(1024)}, bf16[16,40,8,640]{3,2,1,0:T(8,128)(2,1)}, bf16[8,40,2,640]{3,2,1,0:T(2,128)(2,1)}, s32[8]{0:T(128)}) %tuple.11, (bf16[16,40,8,640]{3,2,1,0:T(8,128)(2,1)}, bf16[8,40,2,640]{3,2,1,0:T(2,128)(2,1)}, s32[16]{0:T(128)}, ...), branch_computations={%region_0.0_spmd, %region_1.0_spmd} | conditional | bytes 8 | solution.py:480
  3.4 54.6 %cycle_residual.3 = bf16[16,2,40,640]{3,2,1,0:T(8,128)(2,1)S(1)} custom-call(bf16[16,40,8,640]{3,2,1,0:T(8,128)(2,1)} %get-tuple-element.35.amp_ref, bf16[8,40,2,640]{3,2,1,0:T(2,128)(2,1)} %get-tuple-element.36.w_ref, s32[16]{0:T(128)} %get-tuple-element.37.occ_ref, s32[8]{0:T(128)} %get-tuple-element.38.kocc_ref, s32[640]{0:T(1024)} %get-tuple-element.39.lab_ref.virs_ref, ...), custom_call_target="tpu_custom_call" | custom-call | tf_op jit(solution)/shard_map/cond/branch_1_fun/cycle_residual/pallas_call | solution.py:441
  58.0 2.4 %copy.8 = bf16[16,2,40,640]{3,1,2,0:T(2,128)(2,1)} copy(bf16[16,2,40,640]{3,2,1,0:T(8,128)(2,1)S(1)} %get-tuple-element.41) | data formatting | bytes 3276800 | tf_op jit(solution)/shard_map/cond | solution.py:480
